TPU v7x, 512 devices: a whole 4x8x8 slice. The times are simulated.
512 devices in a mesh: rep: 16 (over y_hi, x, core), fsdp: 32 (over z, y_lo).
Axes of the slice: x: 4, y: 8 (y_hi: 2, y_lo: 4; y = y_hi * 4 + y_lo), z: 8, core: 2. Of those that a mesh axis runs over, the one named last changes fastest.
Arguments:
- grads: float32 [16, 256, 16384], P('rep', 'fsdp'), may hold values from -6 to 6
- master: float32 [256, 16384], P('fsdp'), may hold values from -6 to 6
- moment_one: float32 [256, 16384], P('fsdp'), may hold values from -2 to 2
- moment_two: float32 [256, 16384], P('fsdp'), may hold values from 0.05 to 2
Outputs:
- new_master: float32 [256, 16384], P('fsdp')
- new_one: float32 [256, 16384], P('fsdp')
- new_two: float32 [256, 16384], P('fsdp')
- rollout: bfloat16 [256, 16384], P(None, 'fsdp')
All inputs are finite; a program needn't handle non-finite values.
Results may differ from a plain program's by a relative error of at most 0.0025.
Values may be sent and summed in bfloat16 or wider, within the bound.
No kernel may reach another device: no remote copies, remote signals or barrier semaphores. Data moves between devices by JAX's collectives and lax.ppermute only.
A program may use at most 64 MiB of HBM per device.

v0:
```python
import jax
import jax.numpy as jnp
from jax import lax
from jax.sharding import PartitionSpec as P

STEP = 10


def adamw(mean_grad, master, moment_one, moment_two):
    new_one = 0.9 * moment_one + 0.1 * mean_grad
    new_two = 0.95 * moment_two + 0.05 * mean_grad * mean_grad
    corrected_one = new_one / (1.0 - 0.9**STEP)
    corrected_two = new_two / (1.0 - 0.95**STEP)
    new_master = master - 0.02 * (corrected_one / (jnp.sqrt(corrected_two) + 1e-08) + 0.1 * master)
    return (new_master, new_one, new_two)


def local(grads, master, moment_one, moment_two):
    row_count, full_width = master.shape
    fsdp_count = lax.axis_size("fsdp")
    rep_count = lax.axis_size("rep")
    piece_width = full_width // fsdp_count
    block_count = 1
    block_width = piece_width // block_count

    def columns(source):
        viewed = source.reshape(row_count, fsdp_count, piece_width)
        return viewed.reshape(row_count, fsdp_count * block_width)

    masters, firsts, seconds, rollouts = ([], [], [], [])
    grad_block = columns(grads[0])
    master_block = columns(master)
    first_block = columns(moment_one)
    second_block = columns(moment_two)
    mean_grad = lax.psum(grad_block.astype(jnp.bfloat16), "rep").astype(jnp.float32) / rep_count
    new_master, new_one, new_two = adamw(mean_grad, master_block, first_block, second_block)
    fresh = lax.all_to_all(
        new_master.astype(jnp.bfloat16), "fsdp", split_axis=1, concat_axis=0, tiled=True
    )
    masters.append(new_master.reshape(row_count, fsdp_count, block_width))
    firsts.append(new_one.reshape(row_count, fsdp_count, block_width))
    seconds.append(new_two.reshape(row_count, fsdp_count, block_width))
    rollouts.append(fresh)

    def assemble(pieces):
        return pieces[0].reshape(row_count, full_width)

    rollout = rollouts[0]
    return (assemble(masters), assemble(firsts), assemble(seconds), rollout)


def solution(mesh):
    placed = (P("rep", "fsdp", None), P("fsdp", None), P("fsdp", None), P("fsdp", None))
    return jax.shard_map(
        local,
        mesh=mesh,
        in_specs=placed,
        out_specs=(P("fsdp", None), P("fsdp", None), P("fsdp", None), P(None, "fsdp")),
        check_vma=False,
    )
```

profile of v0, /device:TPU:7, one launch (start us, length us, event | category | flops | bytes accessed | tf_op | source)
XLA Modules:
  0.0 229.1 jit_solution(11922680237035600617)
XLA Ops:
  7.2 0.0 copy-start.1
  7.2 0.0 copy-start
  7.2 0.0 all-reduce.2.cloned.1.call-start
  7.2 1.8 convert_bitcast_fusion
  9.1 0.0 all-reduce.2.cloned.1.call-update
  9.1 189.1 %all-reduce.2.cloned.1.call-done = bf16[8,16384]{1,0:T(8,128)(2,1)} async-done(((bf16[8,16384]{1,0:T(8,128)(2,1)}), bf16[8,16384]{1,0:T(8,128)(2,1)}) %all-reduce.2.cloned.1.call-update) | async-done | bytes 262160 | tf_op jit(solution)/shard_map/psum | solution.py:35
  198.2 0.0 copy-done.1
  198.2 0.0 copy-done
  198.2 2.5 %fusion.3 = (bf16[8,16384]{1,0:T(8,128)(2,1)S(1)}, f32[8,16384]{1,0:T(8,128)}, f32[8,16384]{1,0:T(8,128)}, f32[8,16384]{1,0:T(8,128)}) fusion(f32[8,16384]{1,0:T(8,128)S(1)} %copy-done, bf16[8,16384]{1,0:T(8,128)(2,1)} %all-reduce.2.cloned.1.call-done, f32[8,16384]{1,0:T(8,128)S(1)} %copy-done.1, f32[8,16384]{1,0:T(8,128)} %param.7), kind=kLoop, calls=%fused_computation.8 | loop fusion | flops 2359296 | bytes 3670016 | tf_op jit(solution)/shard_map/convert_element_type | solution.py:38
  200.8 20.8 %all_to_all.19 = bf16[8,32,512]{2,0,1:T(8,128)(2,1)S(1)} all-to-all(bf16[8,32,512]{2,0,1:T(8,128)(2,1)S(1)} %bitcast.6), channel_id=1, replica_groups=mesh['rep'=16,'fsdp'=32] {'fsdp'}, dimensions={1} | all-to-all | bytes 524288 | tf_op jit(solution)/shard_map/all_to_all | solution.py:37
  221.6 0.7 copy.10
Async XLA Ops:
  7.2 191.1 %copy-start.1 = (f32[8,16384]{1,0:T(8,128)S(1)}, f32[8,16384]{1,0:T(8,128)}, u32[]{:S(2)}) copy-start(f32[8,16384]{1,0:T(8,128)} %param.6) | copy-start | bytes 1572868
  7.2 191.0 %copy-start = (f32[8,16384]{1,0:T(8,128)S(1)}, f32[8,16384]{1,0:T(8,128)}, u32[]{:S(2)}) copy-start(f32[8,16384]{1,0:T(8,128)} %param.5) | copy-start | bytes 1572868
  7.2 191.0 %all-reduce.2.cloned.1.call-start = ((), (), s32[]{:S(2)}) async-start(), calls=%async_computation.1 | async-start | bytes 524288 | tf_op jit(solution)/shard_map/psum | solution.py:35
Sparse Core Ops, SparseCore 0:
  11.5 186.6 all-reduce.1
where the time goes:
time: 229 us
  waiting for transfers between devices  189 us (83%)
  blocking collectives  20.8 us (9%)
  between operations  14 us (6%)
  other arithmetic  4.38 us (2%)
    psum x1, waiting for transfers between devices, local(): lax.psum(grad_block.astype(jnp.bfloat16), 'rep').astype(jnp.float32)  189 us
    all_to_all x1, blocking collectives, local(): lax.all_to_all(new_master.astype(jnp.bfloat16), 'fsdp', split_axis=1, con...  20.8 us
  transfers between devices with their start and end apart: 1, of which 1 were waited for; matrix products, arithmetic and copies ran while one was open for 0% of the time, Pallas kernels for 0%

commit v1 on v0

--- a/solution.py
+++ b/solution.py
@@ -32,7 +32,10 @@
     master_block = columns(master)
     first_block = columns(moment_one)
     second_block = columns(moment_two)
-    mean_grad = lax.psum(grad_block.astype(jnp.bfloat16), "rep").astype(jnp.float32) / rep_count
+    mean_grad = (
+        jnp.sum(lax.all_gather(grad_block.astype(jnp.bfloat16), "rep"), axis=0).astype(jnp.float32)
+        / rep_count
+    )
     new_master, new_one, new_two = adamw(mean_grad, master_block, first_block, second_block)
     fresh = lax.all_to_all(
         new_master.astype(jnp.bfloat16), "fsdp", split_axis=1, concat_axis=0, tiled=True

time: 229 us -> 132 us (0.58)
  waiting for transfers between devices: 189 us -> 90 us
    psum x1 -> x0, waiting for transfers between devices: 189 us -> none  [local(): lax.psum(grad_block.astype(jnp.bfloat16), 'rep').astype(jnp.float32)]
    all_gather x0 -> x1, waiting for transfers between devices: none -> 90 us  [local(): lax.all_gather(grad_block.astype(jnp.bfloat16), 'rep')]
    reduce_sum x0 -> x1, other arithmetic: none -> 2.86 us  [local(): jnp.sum(lax.all_gather(grad_block.astype(jnp.bfloat16), 'rep'), axis=0)]
where the time goes in v1:
time: 132 us; the launch traced here: 130 us
  waiting for transfers between devices  90 us (68%)
  blocking collectives  19 us (14%)
  between operations  14.1 us (11%)
  other arithmetic  6.14 us (5%)
    all_gather x1, waiting for transfers between devices, local(): lax.all_gather(grad_block.astype(jnp.bfloat16), 'rep')  90 us
    all_to_all x1, blocking collectives, local(): lax.all_to_all(new_master.astype(jnp.bfloat16), 'fsdp', split_axis=1, con...  19 us
    reduce_sum x1, other arithmetic, local(): jnp.sum(lax.all_gather(grad_block.astype(jnp.bfloat16), 'rep'), axis=0)  2.86 us
  transfers between devices with their start and end apart: 1, of which 1 were waited for; matrix products, arithmetic and copies ran while one was open for 0% of the time, Pallas kernels for 0%

profile of v1, /device:TPU:7, one launch (start us, length us, event | category | flops | bytes accessed | tf_op | source)
XLA Modules:
  0.0 130.1 jit_solution(13178251562014390095)
XLA Ops:
  7.2 0.0 copy-start.2
  7.2 0.0 copy-start.1
  7.2 0.0 copy-start
  7.2 0.0 all-gather.2.cloned.1.call-start
  7.2 1.9 %convert_element_type.12 = bf16[1,8,16384]{2,1,0:T(8,128)(2,1)} convert(f32[1,8,16384]{2,1,0:T(8,128)} %param.4) | non-fusion elementwise | flops 131072 | bytes 786432 | tf_op jit(solution)/shard_map/convert_element_type | solution.py:36
  9.1 0.0 all-gather.2.cloned.1.call-update
  9.1 90.0 %all-gather.2.cloned.1.call-done = bf16[16,8,16384]{2,1,0:T(8,128)(2,1)} async-done(((bf16[1,8,16384]{2,1,0:T(8,128)(2,1)}), bf16[16,8,16384]{2,1,0:T(8,128)(2,1)}) %all-gather.2.cloned.1.call-update) | async-done | bytes 4194320 | tf_op jit(solution)/shard_map/all_gather | solution.py:36
  99.2 2.9 %reduce_sum.12 = bf16[8,16384]{1,0:T(8,128)(2,1)S(1)} reduce(bf16[16,8,16384]{2,1,0:T(8,128)(2,1)} %all-gather.2.cloned.1.call-done, bf16[]{:T(256)} %constant.7.clone.1), dimensions={0}, to_apply=%region_0.0 | reduce | flops 1966080 | bytes 4456450 | tf_op jit(solution)/shard_map/reduce_sum | solution.py:36
  102.0 0.0 copy-done.2
  102.0 0.0 copy-done.1
  102.0 0.0 copy-done
  102.1 1.4 %fusion.3 = (bf16[8,16384]{1,0:T(8,128)(2,1)S(1)}, f32[8,16384]{1,0:T(8,128)}, f32[8,16384]{1,0:T(8,128)}, f32[8,16384]{1,0:T(8,128)}) fusion(f32[8,16384]{1,0:T(8,128)S(1)} %copy-done, bf16[8,16384]{1,0:T(8,128)(2,1)S(1)} %reduce_sum.12, f32[8,16384]{1,0:T(8,128)S(1)} %copy-done.1, f32[8,16384]{1,0:T(8,128)S(1)} %copy-done.2), kind=kLoop, calls=%fused_computation.7 | loop fusion | flops 2359296 | bytes 3670016 | tf_op jit(solution)/shard_map/convert_element_type | solution.py:41
  103.5 19.0 %all_to_all.19 = bf16[8,32,512]{2,0,1:T(8,128)(2,1)S(1)} all-to-all(bf16[8,32,512]{2,0,1:T(8,128)(2,1)S(1)} %bitcast.4), channel_id=1, replica_groups=mesh['rep'=16,'fsdp'=32] {'fsdp'}, dimensions={1} | all-to-all | bytes 524288 | tf_op jit(solution)/shard_map/all_to_all | solution.py:40
  122.5 0.7 copy.9
Async XLA Ops:
  7.2 94.9 %copy-start.2 = (f32[8,16384]{1,0:T(8,128)S(1)}, f32[8,16384]{1,0:T(8,128)}, u32[]{:S(2)}) copy-start(f32[8,16384]{1,0:T(8,128)} %param.7) | copy-start | bytes 1572868
  7.2 94.9 %copy-start.1 = (f32[8,16384]{1,0:T(8,128)S(1)}, f32[8,16384]{1,0:T(8,128)}, u32[]{:S(2)}) copy-start(f32[8,16384]{1,0:T(8,128)} %param.6) | copy-start | bytes 1572868
  7.2 94.9 %copy-start = (f32[8,16384]{1,0:T(8,128)S(1)}, f32[8,16384]{1,0:T(8,128)}, u32[]{:S(2)}) copy-start(f32[8,16384]{1,0:T(8,128)} %param.5) | copy-start | bytes 1572868
  7.2 92.0 %all-gather.2.cloned.1.call-start = ((), (), s32[]{:S(2)}) async-start(), calls=%async_computation.1 | async-start | bytes 4456448 | tf_op jit(solution)/shard_map/all_gather | solution.py:36
Sparse Core Ops, SparseCore 0:
  11.9 87.1 all-gather.1

commit v2 on v0

--- a/solution.py
+++ b/solution.py
@@ -34,8 +34,14 @@
     second_block = columns(moment_two)
     mean_grad = lax.psum(grad_block.astype(jnp.bfloat16), "rep").astype(jnp.float32) / rep_count
     new_master, new_one, new_two = adamw(mean_grad, master_block, first_block, second_block)
-    fresh = lax.all_to_all(
-        new_master.astype(jnp.bfloat16), "fsdp", split_axis=1, concat_axis=0, tiled=True
+    fresh = jnp.concatenate(
+        lax.all_to_all(
+            jnp.stack(jnp.split(new_master.astype(jnp.bfloat16), lax.axis_size("fsdp"), axis=1)),
+            "fsdp",
+            0,
+            0,
+        ),
+        axis=0,
     )
     masters.append(new_master.reshape(row_count, fsdp_count, block_width))
     firsts.append(new_one.reshape(row_count, fsdp_count, block_width))

time: 229 us -> 230 us (level)
  no operation moved by 1% of the time
where the time goes in v2:
time: 230 us; the launch traced here: 229 us
  waiting for transfers between devices  189 us (82%)
  blocking collectives  20.8 us (9%)
  between operations  14.3 us (6%)
  other arithmetic  4.38 us (2%)
    psum x1, waiting for transfers between devices, local(): lax.psum(grad_block.astype(jnp.bfloat16), 'rep').astype(jnp.float32)  189 us
    all_to_all x1, blocking collectives, local(): lax.all_to_all(jnp.stack(jnp.split(new_master.astype(jnp.bfloat16), lax.a...  20.8 us
  transfers between devices with their start and end apart: 1, of which 1 were waited for; matrix products, arithmetic and copies ran while one was open for 0% of the time, Pallas kernels for 0%

profile of v2, /device:TPU:7, one launch (start us, length us, event | category | flops | bytes accessed | tf_op | source)
XLA Modules:
  0.0 229.5 jit_solution(13532089674537964376)
XLA Ops:
  7.2 0.0 copy-start.1
  7.2 0.0 copy-start
  7.2 0.0 all-reduce.2.cloned.1.call-start
  7.2 1.8 convert_bitcast_fusion
  9.1 0.0 all-reduce.2.cloned.1.call-update
  9.1 189.1 %all-reduce.2.cloned.1.call-done = bf16[8,16384]{1,0:T(8,128)(2,1)} async-done(((bf16[8,16384]{1,0:T(8,128)(2,1)}), bf16[8,16384]{1,0:T(8,128)(2,1)}) %all-reduce.2.cloned.1.call-update) | async-done | bytes 262160 | tf_op jit(solution)/shard_map/psum | solution.py:35
  198.2 0.0 copy-done.1
  198.2 0.0 copy-done
  198.2 2.5 %fusion.3 = (bf16[8,16384]{1,0:T(8,128)(2,1)S(1)}, f32[8,16384]{1,0:T(8,128)}, f32[8,16384]{1,0:T(8,128)}, f32[8,16384]{1,0:T(8,128)}) fusion(f32[8,16384]{1,0:T(8,128)S(1)} %copy-done, bf16[8,16384]{1,0:T(8,128)(2,1)} %all-reduce.2.cloned.1.call-done, f32[8,16384]{1,0:T(8,128)S(1)} %copy-done.1, f32[8,16384]{1,0:T(8,128)} %param.7), kind=kLoop, calls=%fused_computation.72 | loop fusion | flops 2359296 | bytes 3670016 | tf_op jit(solution)/shard_map/convert_element_type | solution.py:39
  201.1 20.8 %all_to_all.5 = bf16[32,8,512]{2,1,0:T(8,128)(2,1)S(1)} all-to-all(bf16[32,8,512]{2,1,0:T(8,128)(2,1)S(1)} %constant_dynamic-update-slice_fusion), channel_id=1, replica_groups=mesh['rep'=16,'fsdp'=32] {'fsdp'}, dimensions={0} | all-to-all | bytes 524288 | tf_op jit(solution)/shard_map/all_to_all | solution.py:38
  221.9 0.7 copy.41
  (32 shorter events, 0.1 us)
Async XLA Ops:
  7.2 191.1 %copy-start.1 = (f32[8,16384]{1,0:T(8,128)S(1)}, f32[8,16384]{1,0:T(8,128)}, u32[]{:S(2)}) copy-start(f32[8,16384]{1,0:T(8,128)} %param.6) | copy-start | bytes 1572868
  7.2 191.0 %copy-start = (f32[8,16384]{1,0:T(8,128)S(1)}, f32[8,16384]{1,0:T(8,128)}, u32[]{:S(2)}) copy-start(f32[8,16384]{1,0:T(8,128)} %param.5) | copy-start | bytes 1572868
  7.2 191.0 %all-reduce.2.cloned.1.call-start = ((), (), s32[]{:S(2)}) async-start(), calls=%async_computation.1 | async-start | bytes 524288 | tf_op jit(solution)/shard_map/psum | solution.py:35
Sparse Core Ops, SparseCore 0:
  11.5 186.6 all-reduce.1
